TPU v7x, 32 devices: a whole 2x2x4 slice. The times are simulated.
32 devices in a mesh: rot: 4 (over y, x), space: 8 (over z, core).
Axes of the slice: x: 2, y: 2, z: 4, core: 2. Of those that a mesh axis runs over, the one named last changes fastest.
Arguments:
- raster: bfloat16 [4, 128, 2, 256], P(None, 'space'), may hold values from -6 to 6
- coarse_features: bfloat16 [4, 64, 128, 2, 256], P('rot', None, 'space'), may hold values from -6 to 6
- lift_weight: bfloat16 [4, 9, 64, 4], P('rot'), may hold values from -1 to 1
- lift_bias: float32 [64], replicated, may hold values from -3 to 3
- group_weight: bfloat16 [4, 9, 64, 64], P('rot'), may hold values from -0.125 to 0.125
- group_bias: float32 [64], replicated, may hold values from -3 to 3
Outputs:
- features: bfloat16 [4, 64, 128, 2, 256], P('rot', None, 'space')
All inputs are finite; a program needn't handle non-finite values.
Results may differ from a plain program's by a relative error of at most 0.0045.
Values may be sent and summed in bfloat16 or wider, within the bound.
A program may use at most 192 MiB of HBM per device.

v0:
```python
import jax
import jax.numpy as jnp
from jax import lax
from jax.sharding import PartitionSpec as P


def padded_2(array, sides, width):
    for axis, dim in sides:
        size, length = (lax.axis_size(axis), array.shape[dim])
        up = [(i, (i + 1) % size) for i in range(size - 1)]
        down = [(j, i) for i, j in up]
        last = lax.slice_in_dim(array, length - width, length, axis=dim)
        leading = lax.slice_in_dim(array, 0, width, axis=dim)
        before = lax.ppermute(last, axis, up)
        after = lax.ppermute(leading, axis, down)
        array = jnp.concatenate([before, array, after], axis=dim)
    return array


def passed_along(array, axis, by):
    size = lax.axis_size(axis)
    return lax.ppermute(array, axis, [(i, (i + by) % size) for i in range(size)])


def tap_stack(padded):
    row_count = padded.shape[1] - 2
    col_count = padded.shape[3]
    widened = jnp.pad(padded, ((0, 0), (0, 0), (0, 0), (1, 1)))
    return jnp.stack(
        [
            widened[:, shift_row : shift_row + row_count, :, shift_col : shift_col + col_count]
            for shift_row in range(3)
            for shift_col in range(3)
        ],
        0,
    )


def add_taps(total, weight, padded):
    tile_count = padded.shape[2]
    block_size = min(8, tile_count)

    def one_block(block_index, running):
        tile_term = jnp.einsum(
            "koc,kcrtw->ortw", weight, tap_stack(padded), preferred_element_type=jnp.float32
        )
        return running + tile_term

    return lax.fori_loop(0, tile_count // block_size, one_block, total)


def slice_rimmed(values):
    return padded_2(values, (("space", 1),), 1)


def shards(raster, coarse_features, lift_weight, lift_bias, group_weight, group_bias):
    rot_count = lax.axis_size("rot")
    raster_padded = padded_2(raster, (("space", 1),), 1)
    channels = lift_weight.shape[2]
    shape_out = (channels, raster.shape[1], raster.shape[2], raster.shape[3])
    empty = jnp.zeros(shape_out, jnp.float32)
    lifted = add_taps(empty, lift_weight[0], raster_padded)
    lifted = lifted + lift_bias[:, None, None, None] + coarse_features[0].astype(jnp.float32)
    hidden = jnp.maximum(lifted, 0.0).astype(jnp.bfloat16)
    filters = lax.all_gather(group_weight, "rot", axis=0, tiled=True)
    total = add_taps(empty, filters[0], slice_rimmed(hidden))
    travel = hidden
    for cycle_step in range(1, rot_count):
        travel = passed_along(travel, "rot", 1)
        total = add_taps(total, filters[cycle_step], slice_rimmed(travel))
    result = jnp.maximum(total + group_bias[:, None, None, None], 0.0).astype(jnp.bfloat16)
    return result[None]


def solution(mesh):
    return jax.shard_map(
        shards,
        mesh=mesh,
        in_specs=(
            P(None, "space", None, None),
            P("rot", None, "space", None, None),
            P("rot", None, None, None),
            P(),
            P("rot", None, None, None),
            P(),
        ),
        out_specs=P("rot", None, "space", None, None),
        check_vma=False,
    )
```

profile of v0, /device:TPU:1, one launch (start us, length us, event | category | flops | bytes accessed | tf_op | source)
XLA Modules:
  0.0 140.1 jit_solution(9306880257373840821)
XLA Ops:
  0.0 0.9 copy.169
  1.0 4.6 %collective-permute-start = (bf16[4,1,2,256]{3,1,2,0:T(2,128)(2,1)S(1)}, bf16[4,1,2,256]{3,1,2,0:T(2,128)(2,1)S(1)}, u32[]{:S(2)}, u32[]{:S(2)}) collective-permute-start(bf16[4,1,2,256]{3,1,2,0:T(2,128)(2,1)S(1)} %get-tuple-element.75), channel_id=1, source_target_pairs={{0,1},{1,2},{2,3},{3,4},{4,5},{5,6},{6,7},{8,9},{9,10},{10,11},{11... | collective-permute-start | bytes 12296 | tf_op jit(solution)/shard_map/ppermute | solution.py:14
  5.6 1.9 %collective-permute-start.1 = (bf16[4,1,2,256]{3,1,2,0:T(2,128)(2,1)S(1)}, bf16[4,1,2,256]{3,1,2,0:T(2,128)(2,1)S(1)}, u32[]{:S(2)}, u32[]{:S(2)}) collective-permute-start(bf16[4,1,2,256]{3,1,2,0:T(2,128)(2,1)S(1)} %get-tuple-element.80), channel_id=1, source_target_pairs={{1,0},{2,1},{3,2},{4,3},{5,4},{6,5},{7,6},{9,8},{10,9},{11,10},{12... | collective-permute-start | bytes 12296 | tf_op jit(solution)/shard_map/ppermute | solution.py:15
  7.5 0.9 copy.179
  8.5 2.1 %collective-permute-done.1 = bf16[4,1,2,256]{3,1,2,0:T(2,128)(2,1)S(1)} collective-permute-done((bf16[4,1,2,256]{3,1,2,0:T(2,128)(2,1)S(1)}, bf16[4,1,2,256]{3,1,2,0:T(2,128)(2,1)S(1)}, u32[]{:S(2)}, u32[]{:S(2)}) %collective-permute-start.1) | collective-permute-done | bytes 4128 | tf_op jit(solution)/shard_map/ppermute | solution.py:15
  10.6 0.1 fusion.60
  10.7 0.1 slice_bitcast_fusion.32
  10.8 0.1 copy.175
  11.0 0.1 copy.177
  11.2 0.1 copy.180
  11.4 0.1 copy.183
  11.8 1.8 %stack.209 = bf16[9,4,16,2,256]{4,0,1,3,2:T(8,128)(2,1)S(1)} concatenate(bf16[1,4,16,2,256]{4,0,1,3,2:T(2,128)(2,1)S(1)} %copy.175, bf16[1,4,16,2,256]{4,0,1,3,2:T(2,128)(2,1)S(1)} %copy.176, bf16[1,4,16,2,256]{4,0,1,3,2:T(2,128)(2,1)S(1)} %copy.177, bf16[1,4,16,2,256]{4,0,1,3,2:T(2,128)(2,1)S(1)} %copy.178, bf16[1,4,16,2,256]{4,0,1,3,2:T(2,128)(2,1)S(1)} %copy.179, ...), dimensions={0} | concatenate | bytes 1179648 | tf_op jit(solution)/shard_map/while/body/eval_jaxpr/stack | solution.py:29
  13.7 1.1 fusion.10
  14.8 1.9 %collective-permute-start.2 = (bf16[64,1,2,256]{3,0,2,1:T(8,128)(2,1)S(1)}, bf16[64,1,2,256]{3,0,2,1:T(8,128)(2,1)S(1)}, u32[]{:S(2)}, u32[]{:S(2)}) collective-permute-start(bf16[64,1,2,256]{3,0,2,1:T(8,128)(2,1)S(1)} %get-tuple-element.43), channel_id=1, source_target_pairs={{0,1},{1,2},{2,3},{3,4},{4,5},{5,6},{6,7},{8,9},{9,10},{10,11},{11... | collective-permute-start | bytes 196616 | tf_op jit(solution)/shard_map/ppermute | solution.py:14
  16.7 2.4 %collective-permute-start.3 = (bf16[64,1,2,256]{3,0,2,1:T(8,128)(2,1)S(1)}, bf16[64,1,2,256]{3,0,2,1:T(8,128)(2,1)S(1)}, u32[]{:S(2)}, u32[]{:S(2)}) collective-permute-start(bf16[64,1,2,256]{3,0,2,1:T(8,128)(2,1)S(1)} %get-tuple-element.48), channel_id=1, source_target_pairs={{1,0},{2,1},{3,2},{4,3},{5,4},{6,5},{7,6},{9,8},{10,9},{11,10},{12... | collective-permute-start | bytes 196616 | tf_op jit(solution)/shard_map/ppermute | solution.py:15
  19.1 10.4 %all_gather.3 = bf16[4,9,64,64]{3,2,1,0:T(8,128)(2,1)S(1)} all-gather(bf16[1,9,64,64]{3,2,1,0:T(8,128)(2,1)S(1)} %copy-done.1), channel_id=1, replica_groups=mesh['rot'=4,'space'=8] {'rot'}, dimensions={0}, use_global_device_ids=true | all-gather | bytes 368640 | tf_op jit(solution)/shard_map/all_gather | solution.py:65
  29.5 1.2 collective-permute-start.4
  30.8 1.1 select_maximum_fusion.6
  31.9 0.1 fusion.52
  32.0 0.4 fusion.50
  32.6 0.1 bitcast_dynamic-update-slice_fusion.3
  32.7 0.4 fusion.48
  33.2 0.1 fusion.46
  33.3 0.4 fusion.44
  33.8 20.4 %collective-permute-done.4 = bf16[64,16,2,256]{3,0,2,1:T(8,128)(2,1)S(1)} collective-permute-done((bf16[64,16,2,256]{3,0,2,1:T(8,128)(2,1)S(1)}, bf16[64,16,2,256]{3,0,2,1:T(8,128)(2,1)S(1)}, u32[]{:S(2)}, u32[]{:S(2)}) %collective-permute-start.4) | collective-permute-done | bytes 1048608 | tf_op jit(solution)/shard_map/ppermute | solution.py:22
  54.2 4.2 %collective-permute-start.5 = (bf16[64,1,2,256]{3,0,2,1:T(8,128)(2,1)S(1)}, bf16[64,1,2,256]{3,0,2,1:T(8,128)(2,1)S(1)}, u32[]{:S(2)}, u32[]{:S(2)}) collective-permute-start(bf16[64,1,2,256]{3,0,2,1:T(8,128)(2,1)S(1)} %get-tuple-element.49), channel_id=1, source_target_pairs={{0,1},{1,2},{2,3},{3,4},{4,5},{5,6},{6,7},{8,9},{9,10},{10,11},{11... | collective-permute-start | bytes 196616 | tf_op jit(solution)/shard_map/ppermute | solution.py:14
  58.4 1.9 %collective-permute-start.6 = (bf16[64,1,2,256]{3,0,2,1:T(8,128)(2,1)S(1)}, bf16[64,1,2,256]{3,0,2,1:T(8,128)(2,1)S(1)}, u32[]{:S(2)}, u32[]{:S(2)}) collective-permute-start(bf16[64,1,2,256]{3,0,2,1:T(8,128)(2,1)S(1)} %get-tuple-element.50), channel_id=1, source_target_pairs={{1,0},{2,1},{3,2},{4,3},{5,4},{6,5},{7,6},{9,8},{10,9},{11,10},{12... | collective-permute-start | bytes 196616 | tf_op jit(solution)/shard_map/ppermute | solution.py:15
  60.4 1.9 %fusion.6 = f32[16,2,256,64,1]{2,3,0,1,4:T(8,128)S(1)} fusion(bf16[9,64,16,2,256]{4,1,3,2,0:T(8,128)(2,1)S(1)} %fusion.44, bf16[4,9,64,64]{3,2,1,0:T(8,128)(2,1)S(1)} %all_gather.3), kind=kOutput, calls=%fused_computation.6 | convolution fusion | flops 603979776 | bytes 11681792 | tf_op jit(solution)/shard_map/while/body/eval_jaxpr/koc,kcrtw->ortw/dot_general | solution.py:44
  62.3 0.4 collective-permute-start.7
  62.6 1.4 collective-permute-done.6
  64.0 1.1 select_maximum_fusion.4
  65.2 0.1 fusion.42
  65.3 0.4 fusion.40
  65.8 0.1 bitcast_dynamic-update-slice_fusion.2
  65.9 0.4 fusion.38
  66.5 0.1 fusion.36
  66.6 0.4 fusion.34
  67.0 19.8 %collective-permute-done.7 = bf16[64,16,2,256]{3,0,2,1:T(8,128)(2,1)S(1)} collective-permute-done((bf16[64,16,2,256]{3,0,2,1:T(8,128)(2,1)S(1)}, bf16[64,16,2,256]{3,0,2,1:T(8,128)(2,1)S(1)}, u32[]{:S(2)}, u32[]{:S(2)}) %collective-permute-start.7) | collective-permute-done | bytes 1048608 | tf_op jit(solution)/shard_map/ppermute | solution.py:22
  86.8 5.1 %collective-permute-start.8 = (bf16[64,1,2,256]{3,0,2,1:T(8,128)(2,1)S(1)}, bf16[64,1,2,256]{3,0,2,1:T(8,128)(2,1)S(1)}, u32[]{:S(2)}, u32[]{:S(2)}) collective-permute-start(bf16[64,1,2,256]{3,0,2,1:T(8,128)(2,1)S(1)} %get-tuple-element.51), channel_id=1, source_target_pairs={{0,1},{1,2},{2,3},{3,4},{4,5},{5,6},{6,7},{8,9},{9,10},{10,11},{11... | collective-permute-start | bytes 196616 | tf_op jit(solution)/shard_map/ppermute | solution.py:14
  91.9 2.1 %collective-permute-start.9 = (bf16[64,1,2,256]{3,0,2,1:T(8,128)(2,1)S(1)}, bf16[64,1,2,256]{3,0,2,1:T(8,128)(2,1)S(1)}, u32[]{:S(2)}, u32[]{:S(2)}) collective-permute-start(bf16[64,1,2,256]{3,0,2,1:T(8,128)(2,1)S(1)} %get-tuple-element.56), channel_id=1, source_target_pairs={{1,0},{2,1},{3,2},{4,3},{5,4},{6,5},{7,6},{9,8},{10,9},{11,10},{12... | collective-permute-start | bytes 196616 | tf_op jit(solution)/shard_map/ppermute | solution.py:15
  94.0 1.9 %fusion.4 = f32[16,2,256,64,1]{2,3,0,1,4:T(8,128)S(1)} fusion(bf16[9,64,16,2,256]{4,1,3,2,0:T(8,128)(2,1)S(1)} %fusion.34, bf16[4,9,64,64]{3,2,1,0:T(8,128)(2,1)S(1)} %all_gather.3), kind=kOutput, calls=%fused_computation.4 | convolution fusion | flops 603979776 | bytes 11681792 | tf_op jit(solution)/shard_map/while/body/eval_jaxpr/koc,kcrtw->ortw/dot_general | solution.py:44
  96.0 1.8 %collective-permute-done.9 = bf16[64,1,2,256]{3,0,2,1:T(8,128)(2,1)S(1)} collective-permute-done((bf16[64,1,2,256]{3,0,2,1:T(8,128)(2,1)S(1)}, bf16[64,1,2,256]{3,0,2,1:T(8,128)(2,1)S(1)}, u32[]{:S(2)}, u32[]{:S(2)}) %collective-permute-start.9) | collective-permute-done | bytes 65568 | tf_op jit(solution)/shard_map/ppermute | solution.py:15
  97.8 1.1 select_maximum_fusion.2
  99.0 0.1 fusion.32
  99.1 0.4 fusion.30
  99.6 0.1 bitcast_dynamic-update-slice_fusion.1
  99.7 0.4 fusion.28
  100.2 0.1 fusion.26
  100.4 0.4 fusion.24
  100.8 18.2 %collective-permute-done.10 = bf16[64,16,2,256]{3,0,2,1:T(8,128)(2,1)S(1)} collective-permute-done((bf16[64,16,2,256]{3,0,2,1:T(8,128)(2,1)S(1)}, bf16[64,16,2,256]{3,0,2,1:T(8,128)(2,1)S(1)}, u32[]{:S(2)}, u32[]{:S(2)}) %collective-permute-start.10) | collective-permute-done | bytes 1048608 | tf_op jit(solution)/shard_map/ppermute | solution.py:22
  119.0 7.5 %collective-permute-start.11 = (bf16[64,1,2,256]{3,0,2,1:T(8,128)(2,1)S(1)}, bf16[64,1,2,256]{3,0,2,1:T(8,128)(2,1)S(1)}, u32[]{:S(2)}, u32[]{:S(2)}) collective-permute-start(bf16[64,1,2,256]{3,0,2,1:T(8,128)(2,1)S(1)} %get-tuple-element.57), channel_id=1, source_target_pairs={{0,1},{1,2},{2,3},{3,4},{4,5},{5,6},{6,7},{8,9},{9,10},{10,11},{11... | collective-permute-start | bytes 196616 | tf_op jit(solution)/shard_map/ppermute | solution.py:14
  126.5 1.9 %collective-permute-start.12 = (bf16[64,1,2,256]{3,0,2,1:T(8,128)(2,1)S(1)}, bf16[64,1,2,256]{3,0,2,1:T(8,128)(2,1)S(1)}, u32[]{:S(2)}, u32[]{:S(2)}) collective-permute-start(bf16[64,1,2,256]{3,0,2,1:T(8,128)(2,1)S(1)} %get-tuple-element.58), channel_id=1, source_target_pairs={{1,0},{2,1},{3,2},{4,3},{5,4},{6,5},{7,6},{9,8},{10,9},{11,10},{12... | collective-permute-start | bytes 196616 | tf_op jit(solution)/shard_map/ppermute | solution.py:15
  128.5 1.9 %fusion.2 = f32[16,2,256,64,1]{2,3,0,1,4:T(8,128)S(1)} fusion(bf16[9,64,16,2,256]{4,1,3,2,0:T(8,128)(2,1)S(1)} %fusion.24, bf16[4,9,64,64]{3,2,1,0:T(8,128)(2,1)S(1)} %all_gather.3), kind=kOutput, calls=%fused_computation.2 | convolution fusion | flops 603979776 | bytes 11681792 | tf_op jit(solution)/shard_map/while/body/eval_jaxpr/koc,kcrtw->ortw/dot_general | solution.py:44
  130.4 1.7 %collective-permute-done.12 = bf16[64,1,2,256]{3,0,2,1:T(8,128)(2,1)S(1)} collective-permute-done((bf16[64,1,2,256]{3,0,2,1:T(8,128)(2,1)S(1)}, bf16[64,1,2,256]{3,0,2,1:T(8,128)(2,1)S(1)}, u32[]{:S(2)}, u32[]{:S(2)}) %collective-permute-start.12) | collective-permute-done | bytes 65568 | tf_op jit(solution)/shard_map/ppermute | solution.py:15
  132.1 1.1 select_maximum_fusion
  133.3 0.1 fusion.22
  133.4 0.4 fusion.20
  133.9 0.1 bitcast_dynamic-update-slice_fusion
  134.0 0.4 fusion.18
  134.6 0.1 fusion.16
  134.7 0.4 fusion.14
  135.1 1.9 %fusion = f32[16,2,256,64,1]{2,3,0,1,4:T(8,128)S(1)} fusion(bf16[9,64,16,2,256]{4,1,3,2,0:T(8,128)(2,1)S(1)} %fusion.14, bf16[4,9,64,64]{3,2,1,0:T(8,128)(2,1)S(1)} %all_gather.3), kind=kOutput, calls=%fused_computation | convolution fusion | flops 603979776 | bytes 11681792 | tf_op jit(solution)/shard_map/while/body/eval_jaxpr/koc,kcrtw->ortw/dot_general | solution.py:44
  137.1 1.0 fusion.54
  138.1 2.1 %copy.186 = bf16[1,64,16,2,256]{4,3,2,1,0:T(2,128)(2,1)} copy(bf16[1,64,16,2,256]{4,1,3,2,0:T(8,128)(2,1)S(1)} %fusion.54) | data formatting | bytes 2097152 | tf_op jit(solution)/shard_map/broadcast_in_dim | solution.py:72
  (39 shorter events, 1.5 us)
Async XLA Ops:
  0.0 13.6 %copy-start = (bf16[1,9,64,4]{2,3,1,0:T(4,128)(2,1)S(1)}, bf16[1,9,64,4]{2,3,1,0:T(4,128)(2,1)}, u32[]{:S(2)}) copy-start(bf16[1,9,64,4]{2,3,1,0:T(4,128)(2,1)} %param.8) | copy-start | bytes 13828
  0.0 13.6 %copy-start.3 = (bf16[1,64,16,2,256]{4,3,2,1,0:T(2,128)(2,1)S(1)}, bf16[1,64,16,2,256]{4,3,2,1,0:T(2,128)(2,1)}, u32[]{:S(2)}) copy-start(bf16[1,64,16,2,256]{4,3,2,1,0:T(2,128)(2,1)} %param.7) | copy-start | bytes 3145732
  0.0 13.7 %copy-start.4 = (f32[64]{0:T(128)S(1)}, f32[64]{0:T(128)}, u32[]{:S(2)}) copy-start(f32[64]{0:T(128)} %param.9) | copy-start | bytes 772
  1.0 7.5 %collective-permute-start = (bf16[4,1,2,256]{3,1,2,0:T(2,128)(2,1)S(1)}, bf16[4,1,2,256]{3,1,2,0:T(2,128)(2,1)S(1)}, u32[]{:S(2)}, u32[]{:S(2)}) collective-permute-start(bf16[4,1,2,256]{3,1,2,0:T(2,128)(2,1)S(1)} %get-tuple-element.75), channel_id=1, source_target_pairs={{0,1},{1,2},{2,3},{3,4},{4,5},{5,6},{6,7},{8,9},{9,10},{10,11},{11... | collective-permute-start | bytes 12296 | tf_op jit(solution)/shard_map/ppermute | solution.py:14
  5.6 5.0 %collective-permute-start.1 = (bf16[4,1,2,256]{3,1,2,0:T(2,128)(2,1)S(1)}, bf16[4,1,2,256]{3,1,2,0:T(2,128)(2,1)S(1)}, u32[]{:S(2)}, u32[]{:S(2)}) collective-permute-start(bf16[4,1,2,256]{3,1,2,0:T(2,128)(2,1)S(1)} %get-tuple-element.80), channel_id=1, source_target_pairs={{1,0},{2,1},{3,2},{4,3},{5,4},{6,5},{7,6},{9,8},{10,9},{11,10},{12... | collective-permute-start | bytes 12296 | tf_op jit(solution)/shard_map/ppermute | solution.py:15
  11.3 7.8 %copy-start.1 = (bf16[1,9,64,64]{3,2,1,0:T(8,128)(2,1)S(1)}, bf16[1,9,64,64]{3,2,1,0:T(8,128)(2,1)}, u32[]{:S(2)}) copy-start(bf16[1,9,64,64]{3,2,1,0:T(8,128)(2,1)} %param.10) | copy-start | bytes 221188
  14.8 16.0 %collective-permute-start.2 = (bf16[64,1,2,256]{3,0,2,1:T(8,128)(2,1)S(1)}, bf16[64,1,2,256]{3,0,2,1:T(8,128)(2,1)S(1)}, u32[]{:S(2)}, u32[]{:S(2)}) collective-permute-start(bf16[64,1,2,256]{3,0,2,1:T(8,128)(2,1)S(1)} %get-tuple-element.43), channel_id=1, source_target_pairs={{0,1},{1,2},{2,3},{3,4},{4,5},{5,6},{6,7},{8,9},{9,10},{10,11},{11... | collective-permute-start | bytes 196616 | tf_op jit(solution)/shard_map/ppermute | solution.py:14
  16.7 14.0 %collective-permute-start.3 = (bf16[64,1,2,256]{3,0,2,1:T(8,128)(2,1)S(1)}, bf16[64,1,2,256]{3,0,2,1:T(8,128)(2,1)S(1)}, u32[]{:S(2)}, u32[]{:S(2)}) collective-permute-start(bf16[64,1,2,256]{3,0,2,1:T(8,128)(2,1)S(1)} %get-tuple-element.48), channel_id=1, source_target_pairs={{1,0},{2,1},{3,2},{4,3},{5,4},{6,5},{7,6},{9,8},{10,9},{11,10},{12... | collective-permute-start | bytes 196616 | tf_op jit(solution)/shard_map/ppermute | solution.py:15
  29.5 24.7 %collective-permute-start.4 = (bf16[64,16,2,256]{3,0,2,1:T(8,128)(2,1)S(1)}, bf16[64,16,2,256]{3,0,2,1:T(8,128)(2,1)S(1)}, u32[]{:S(2)}, u32[]{:S(2)}) collective-permute-start(bf16[64,16,2,256]{3,0,2,1:T(8,128)(2,1)S(1)} %fusion.10), channel_id=1, source_target_pairs={{0,8},{8,16},{16,24},{24,0},{1,9},{9,17},{17,25},{25,1},{2,10},{10... | collective-permute-start | bytes 3145736 | tf_op jit(solution)/shard_map/ppermute | solution.py:22
  54.2 8.4 %collective-permute-start.5 = (bf16[64,1,2,256]{3,0,2,1:T(8,128)(2,1)S(1)}, bf16[64,1,2,256]{3,0,2,1:T(8,128)(2,1)S(1)}, u32[]{:S(2)}, u32[]{:S(2)}) collective-permute-start(bf16[64,1,2,256]{3,0,2,1:T(8,128)(2,1)S(1)} %get-tuple-element.49), channel_id=1, source_target_pairs={{0,1},{1,2},{2,3},{3,4},{4,5},{5,6},{6,7},{8,9},{9,10},{10,11},{11... | collective-permute-start | bytes 196616 | tf_op jit(solution)/shard_map/ppermute | solution.py:14
  58.4 5.6 %collective-permute-start.6 = (bf16[64,1,2,256]{3,0,2,1:T(8,128)(2,1)S(1)}, bf16[64,1,2,256]{3,0,2,1:T(8,128)(2,1)S(1)}, u32[]{:S(2)}, u32[]{:S(2)}) collective-permute-start(bf16[64,1,2,256]{3,0,2,1:T(8,128)(2,1)S(1)} %get-tuple-element.50), channel_id=1, source_target_pairs={{1,0},{2,1},{3,2},{4,3},{5,4},{6,5},{7,6},{9,8},{10,9},{11,10},{12... | collective-permute-start | bytes 196616 | tf_op jit(solution)/shard_map/ppermute | solution.py:15
  62.3 24.5 %collective-permute-start.7 = (bf16[64,16,2,256]{3,0,2,1:T(8,128)(2,1)S(1)}, bf16[64,16,2,256]{3,0,2,1:T(8,128)(2,1)S(1)}, u32[]{:S(2)}, u32[]{:S(2)}) collective-permute-start(bf16[64,16,2,256]{3,0,2,1:T(8,128)(2,1)S(1)} %collective-permute-done.4), channel_id=1, source_target_pairs={{0,8},{8,16},{16,24},{24,0},{1,9},{9,17},{17,25},{25,1},{2,10},{10... | collective-permute-start | bytes 3145736 | tf_op jit(solution)/shard_map/ppermute | solution.py:22
  86.8 9.2 %collective-permute-start.8 = (bf16[64,1,2,256]{3,0,2,1:T(8,128)(2,1)S(1)}, bf16[64,1,2,256]{3,0,2,1:T(8,128)(2,1)S(1)}, u32[]{:S(2)}, u32[]{:S(2)}) collective-permute-start(bf16[64,1,2,256]{3,0,2,1:T(8,128)(2,1)S(1)} %get-tuple-element.51), channel_id=1, source_target_pairs={{0,1},{1,2},{2,3},{3,4},{4,5},{5,6},{6,7},{8,9},{9,10},{10,11},{11... | collective-permute-start | bytes 196616 | tf_op jit(solution)/shard_map/ppermute | solution.py:14
  91.9 5.9 %collective-permute-start.9 = (bf16[64,1,2,256]{3,0,2,1:T(8,128)(2,1)S(1)}, bf16[64,1,2,256]{3,0,2,1:T(8,128)(2,1)S(1)}, u32[]{:S(2)}, u32[]{:S(2)}) collective-permute-start(bf16[64,1,2,256]{3,0,2,1:T(8,128)(2,1)S(1)} %get-tuple-element.56), channel_id=1, source_target_pairs={{1,0},{2,1},{3,2},{4,3},{5,4},{6,5},{7,6},{9,8},{10,9},{11,10},{12... | collective-permute-start | bytes 196616 | tf_op jit(solution)/shard_map/ppermute | solution.py:15
  95.9 23.0 %collective-permute-start.10 = (bf16[64,16,2,256]{3,0,2,1:T(8,128)(2,1)S(1)}, bf16[64,16,2,256]{3,0,2,1:T(8,128)(2,1)S(1)}, u32[]{:S(2)}, u32[]{:S(2)}) collective-permute-start(bf16[64,16,2,256]{3,0,2,1:T(8,128)(2,1)S(1)} %collective-permute-done.7), channel_id=1, source_target_pairs={{0,8},{8,16},{16,24},{24,0},{1,9},{9,17},{17,25},{25,1},{2,10},{10... | collective-permute-start | bytes 3145736 | tf_op jit(solution)/shard_map/ppermute | solution.py:22
  119.0 11.4 %collective-permute-start.11 = (bf16[64,1,2,256]{3,0,2,1:T(8,128)(2,1)S(1)}, bf16[64,1,2,256]{3,0,2,1:T(8,128)(2,1)S(1)}, u32[]{:S(2)}, u32[]{:S(2)}) collective-permute-start(bf16[64,1,2,256]{3,0,2,1:T(8,128)(2,1)S(1)} %get-tuple-element.57), channel_id=1, source_target_pairs={{0,1},{1,2},{2,3},{3,4},{4,5},{5,6},{6,7},{8,9},{9,10},{10,11},{11... | collective-permute-start | bytes 196616 | tf_op jit(solution)/shard_map/ppermute | solution.py:14
  126.5 5.6 %collective-permute-start.12 = (bf16[64,1,2,256]{3,0,2,1:T(8,128)(2,1)S(1)}, bf16[64,1,2,256]{3,0,2,1:T(8,128)(2,1)S(1)}, u32[]{:S(2)}, u32[]{:S(2)}) collective-permute-start(bf16[64,1,2,256]{3,0,2,1:T(8,128)(2,1)S(1)} %get-tuple-element.58), channel_id=1, source_target_pairs={{1,0},{2,1},{3,2},{4,3},{5,4},{6,5},{7,6},{9,8},{10,9},{11,10},{12... | collective-permute-start | bytes 196616 | tf_op jit(solution)/shard_map/ppermute | solution.py:15
  135.1 1.9 %copy-start.2 = (f32[64]{0:T(128)S(1)}, f32[64]{0:T(128)}, u32[]{:S(2)}) copy-start(f32[64]{0:T(128)} %param.11) | copy-start | bytes 772
where the time goes:
time: 141 us; the launch traced here: 140 us
  waiting for transfers between devices  65.4 us (46%)
  starting transfers between devices  35.3 us (25%)
  local copies, waits for them, and re-layouts  13.4 us (10%)
  blocking collectives  10.4 us (7%)
  matrix products  8.69 us (6%)
  other arithmetic  6.32 us (4%)
    ppermute x3, waiting for transfers between devices, passed_along(): lax.ppermute(array, axis, [(i, (i + by) % size) for i in range(size)])  58.4 us
    ppermute x5, starting transfers between devices, padded_2(): before = lax.ppermute(last, axis, up)  23.4 us
    all_gather x1, blocking collectives, shards(): filters = lax.all_gather(group_weight, 'rot', axis=0, tiled=True)  10.4 us
    ppermute x5, starting transfers between devices, padded_2(): after = lax.ppermute(leading, axis, down)  10.2 us
    dot_general x5, matrix products, one_block(): jnp.einsum('koc,kcrtw->ortw', weight, tap_stack(padded), preferred_elemen...  8.69 us
    ppermute x5, waiting for transfers between devices, padded_2(): after = lax.ppermute(leading, axis, down)  6.98 us
    unnamed x35, local copies, waits for them, and re-layouts  5.82 us
    another operation x15, local copies, waits for them, and re-layouts, tap_stack(): jnp.stack([widened[:, shift_row:shift_row + row_count, :, shift_col:shift...  5.49 us
  transfers between devices with their start and end apart: 13, of which 7 were waited for; matrix products, arithmetic and copies ran while one was open for 11% of the time, Pallas kernels for 0%

commit v1 on v0

v1 whole, which is shorter than its diff:
```python
import functools

import jax
import jax.numpy as jnp
from jax import lax
from jax.experimental import pallas as pl
from jax.experimental.pallas import tpu as pltpu
from jax.sharding import PartitionSpec as P

MESH = pl.DeviceIdType.MESH
STEP = 2


def send_order(chunks):
    inner = list(range(1, chunks - 1))
    return inner[:2] + [0, chunks - 1] + inner[2:]


def mix_order(chunks):
    got, done, plan = set(), set(), []
    for j in send_order(chunks):
        got.add(j)
        ready = [
            i
            for i in range(1, chunks - 1)
            if i not in done and {i - 1, i, i + 1} <= got
        ]
        done.update(ready)
        plan.append((j, ready))
    plan[-1][1].extend([0, chunks - 1])
    return plan


def kernel(
    rots,
    spaces,
    coarse_ref,
    raster_ref,
    lift_ref,
    lift_bias_ref,
    filter_ref,
    group_bias_ref,
    out_ref,
    hid,
    rext,
    filters,
    stacked,
    acc,
    part_out,
    part_in,
    hid_s,
    hid_r,
    up_s,
    up_r,
    down_s,
    down_r,
    ras_s,
    ras_r,
    fil_s,
    fil_r,
    par_s,
    par_r,
):
    g = lax.axis_index("rot")
    s = lax.axis_index("space")
    half = rots // 2
    tiles, rows, ch, cols = coarse_ref.shape
    chunks = rows // STEP
    hi, lo = g // half, lax.rem(g, half)

    def low(k):
        return hi * half + lax.rem(lo + k, half)

    def high(k):
        return lax.rem(g + k * half, rots)

    def gather_group(t):
        return (low, half) if t % 2 == 0 else (high, 2)

    def sum_group(t):
        return (high, 2) if t % 2 == 0 else (low, half)

    has_up = s > 0
    has_down = s < spaces - 1

    def hidden_copy(t, k, j):
        member, n = gather_group(t)
        span = pl.ds(1 + j * STEP, STEP)
        return pltpu.make_async_remote_copy(
            src_ref=hid.at[t, 0, span],
            dst_ref=hid.at[t, n - k, span],
            send_sem=hid_s.at[t, k - 1, j],
            recv_sem=hid_r.at[t, n - k - 1, j],
            device_id=(member(k), s),
            device_id_type=MESH,
        )

    def up_copy(t, k):
        return pltpu.make_async_remote_copy(
            src_ref=hid.at[t, k, 1],
            dst_ref=hid.at[t, k, rows + 1],
            send_sem=up_s.at[t, k],
            recv_sem=up_r.at[t, k],
            device_id=(g, s - 1),
            device_id_type=MESH,
        )

    def down_copy(t, k):
        return pltpu.make_async_remote_copy(
            src_ref=hid.at[t, k, rows],
            dst_ref=hid.at[t, k, 0],
            send_sem=down_s.at[t, k],
            recv_sem=down_r.at[t, k],
            device_id=(g, s + 1),
            device_id_type=MESH,
        )

    def raster_copy(way):
        src, dst, to = ((1, rows + 1, s - 1), (rows, 0, s + 1))[way]
        return pltpu.make_async_remote_copy(
            src_ref=rext.at[src],
            dst_ref=rext.at[dst],
            send_sem=ras_s.at[way],
            recv_sem=ras_r.at[way],
            device_id=(g, to),
            device_id_type=MESH,
        )

    def filter_copy(k):
        return pltpu.make_async_remote_copy(
            src_ref=filter_ref,
            dst_ref=filters.at[rots - k],
            send_sem=fil_s.at[k - 1],
            recv_sem=fil_r.at[rots - k - 1],
            device_id=(lax.rem(g + k, rots), s),
            device_id_type=MESH,
        )

    def part_copy(t, k, j):
        member, n = sum_group(t)
        span = pl.ds(j * STEP, STEP)
        return pltpu.make_async_remote_copy(
            src_ref=part_out.at[t, k - 1, span],
            dst_ref=part_in.at[t, n - k - 1, span],
            send_sem=par_s.at[t, k - 1, j],
            recv_sem=par_r.at[t, n - k - 1, j],
            device_id=(member(k), s),
            device_id_type=MESH,
        )

    barrier = pltpu.get_barrier_semaphore()
    for k in range(1, rots):
        pl.semaphore_signal(barrier, inc=1, device_id=(lax.rem(g + k, rots), s), device_id_type=MESH)

    @pl.when(has_up)
    def _():
        pl.semaphore_signal(barrier, inc=1, device_id=(g, s - 1), device_id_type=MESH)

    @pl.when(has_down)
    def _():
        pl.semaphore_signal(barrier, inc=1, device_id=(g, s + 1), device_id_type=MESH)

    rext[1 : rows + 1] = raster_ref[...]
    zero_row = jnp.zeros((ch, cols), hid.dtype)

    @pl.when(jnp.logical_not(has_up))
    def _():
        rext[0] = jnp.zeros(rext.shape[1:], rext.dtype)
        for t in range(tiles):
            for k in range(gather_group(t)[1]):
                hid[t, k, 0] = zero_row

    @pl.when(jnp.logical_not(has_down))
    def _():
        rext[rows + 1] = jnp.zeros(rext.shape[1:], rext.dtype)
        for t in range(tiles):
            for k in range(gather_group(t)[1]):
                hid[t, k, rows + 1] = zero_row

    around = has_up.astype(jnp.int32) + has_down.astype(jnp.int32)
    pl.semaphore_wait(barrier, rots - 1 + around)

    @pl.when(has_up)
    def _():
        raster_copy(0).start()

    @pl.when(has_down)
    def _():
        raster_copy(1).start()

    def lift_row(r, carry):
        taps = rext[pl.ds(r, 3)].reshape(3 * rext.shape[1], rext.shape[2])
        lifted = jnp.dot(lift_ref[...], taps, preferred_element_type=jnp.float32)
        for t in range(tiles):
            total = lifted[:, t * cols : (t + 1) * cols] + lift_bias_ref[...]
            total = total + coarse_ref[t, r].astype(jnp.float32)
            hid[t, 0, r + 1] = jnp.maximum(total, 0.0).astype(hid.dtype)
        return carry

    for place, j in enumerate(send_order(chunks)):
        if place == 2:

            @pl.when(has_down)
            def _():
                raster_copy(0).wait_recv()

            @pl.when(has_up)
            def _():
                raster_copy(1).wait_recv()

        lax.fori_loop(j * STEP, (j + 1) * STEP, lift_row, 0)
        for t in range(tiles):
            for k in range(1, gather_group(t)[1]):
                hidden_copy(t, k, j).start()
        if place == 1:
            for k in range(1, rots):
                filter_copy(k).start()
        if j == 0:

            @pl.when(has_up)
            def _():
                for t in range(tiles):
                    up_copy(t, 0).start()

        if j == chunks - 1:

            @pl.when(has_down)
            def _():
                for t in range(tiles):
                    down_copy(t, 0).start()

    filters[0] = filter_ref[...]
    for k in range(1, rots):
        filter_copy(k).wait()
    height = filter_ref.shape[0]
    for t in range(tiles):
        take, n_take = gather_group(t)
        give, n_give = sum_group(t)
        for h in range(n_take):
            for p in range(n_give):
                relative = lax.rem(give(p) - take(h) + rots, rots)
                place = lax.rem(relative - g + rots, rots)
                stacked[t, h, p * height : (p + 1) * height] = filters[place]

    lane = lax.broadcasted_iota(jnp.int32, (ch, cols), 1)

    def mix(t, j):
        n_take = gather_group(t)[1]
        n_give = sum_group(t)[1]

        def one_row(r, carry):
            total = None
            for h in range(n_take):
                rim = hid[t, h, pl.ds(r, 3)].reshape(3 * ch, cols)
                term = jnp.dot(
                    stacked[t, h, : n_give * height], rim, preferred_element_type=jnp.float32
                )
                total = term if total is None else total + term
            for p in range(n_give):
                left = total[p * height : p * height + ch]
                mid = total[p * height + ch : p * height + 2 * ch]
                right = total[p * height + 2 * ch : (p + 1) * height]
                left = jnp.where(lane == 0, 0.0, pltpu.roll(left, 1, 1))
                right = jnp.where(lane == cols - 1, 0.0, pltpu.roll(right, cols - 1, 1))
                value = mid + left + right
                if p == 0:
                    acc[t, r] = value + group_bias_ref[...]
                else:
                    part_out[t, p - 1, r] = value.astype(part_out.dtype)
            return carry

        lax.fori_loop(j * STEP, (j + 1) * STEP, one_row, 0)
        for k in range(1, n_give):
            part_copy(t, k, j).start()

    finished = []
    for j, ready in mix_order(chunks):
        for t in range(tiles):
            n_take = gather_group(t)[1]
            for k in range(1, n_take):
                hidden_copy(t, k, j).wait_recv()
            if j == 0:

                @pl.when(has_up)
                def _():
                    for k in range(1, n_take):
                        up_copy(t, k).start()

            if j == chunks - 1:

                @pl.when(has_down)
                def _():
                    for k in range(1, n_take):
                        down_copy(t, k).start()

        for i in ready:
            for t in range(tiles):
                n_take = gather_group(t)[1]
                if i == 0:

                    @pl.when(has_up)
                    def _():
                        for k in range(n_take):
                            down_copy(t, k).wait_recv()

                if i == chunks - 1:

                    @pl.when(has_down)
                    def _():
                        for k in range(n_take):
                            up_copy(t, k).wait_recv()

                mix(t, i)
            finished.append(i)

    for j in finished:
        for t in range(tiles):
            n_give = sum_group(t)[1]
            for k in range(1, n_give):
                part_copy(t, k, j).wait_recv()

            def last_row(r, carry):
                total = acc[t, r]
                for k in range(1, n_give):
                    total = total + part_in[t, k - 1, r].astype(jnp.float32)
                out_ref[t, r] = jnp.maximum(total, 0.0).astype(out_ref.dtype)
                return carry

            lax.fori_loop(j * STEP, (j + 1) * STEP, last_row, 0)

    for t in range(tiles):
        for j in range(chunks):
            for k in range(1, gather_group(t)[1]):
                hidden_copy(t, k, j).wait_send()
            for k in range(1, sum_group(t)[1]):
                part_copy(t, k, j).wait_send()

    @pl.when(has_up)
    def _():
        raster_copy(0).wait_send()
        for t in range(tiles):
            for k in range(gather_group(t)[1]):
                up_copy(t, k).wait_send()

    @pl.when(has_down)
    def _():
        raster_copy(1).wait_send()
        for t in range(tiles):
            for k in range(gather_group(t)[1]):
                down_copy(t, k).wait_send()


def shards(rots, spaces, raster, coarse, lift_weight, lift_bias, group_weight, group_bias):
    ch, cin = lift_weight.shape[2:]
    _, rows, tiles, cols = raster.shape
    half = rots // 2
    most = max(half, 2)
    coarse_in = jnp.transpose(coarse[0], (2, 1, 0, 3))
    wide = jnp.pad(raster, ((0, 0), (0, 0), (0, 0), (1, 1)))
    taps = jnp.stack([wide[..., d : d + cols] for d in range(3)], 0)
    depth = -(-3 * cin // 16) * 16
    taps = jnp.transpose(taps, (2, 0, 1, 3, 4)).reshape(rows, 3 * cin, tiles * cols)
    taps = jnp.pad(taps, ((0, 0), (0, depth - 3 * cin), (0, 0)))
    lift = jnp.transpose(lift_weight[0].reshape(3, 3, ch, cin), (2, 0, 1, 3)).reshape(ch, 3, 3 * cin)
    lift = jnp.pad(lift, ((0, 0), (0, 0), (0, depth - 3 * cin))).reshape(ch, 3 * depth)
    filt = jnp.transpose(group_weight[0].reshape(3, 3, ch, ch), (1, 2, 0, 3)).reshape(3 * ch, 3 * ch)
    bf16, f32 = jnp.bfloat16, jnp.float32
    chunks = rows // STEP
    dma = pltpu.SemaphoreType.DMA
    out = pl.pallas_call(
        functools.partial(kernel, rots, spaces),
        out_shape=jax.ShapeDtypeStruct((tiles, rows, ch, cols), bf16),
        in_specs=[pl.BlockSpec(memory_space=pltpu.VMEM)] * 6,
        out_specs=pl.BlockSpec(memory_space=pltpu.VMEM),
        scratch_shapes=[
            pltpu.VMEM((tiles, most, rows + 2, ch, cols), bf16),
            pltpu.VMEM((rows + 2, depth, tiles * cols), bf16),
            pltpu.VMEM((rots, 3 * ch, 3 * ch), bf16),
            pltpu.VMEM((tiles, most, most * 3 * ch, 3 * ch), bf16),
            pltpu.VMEM((tiles, rows, ch, cols), f32),
            pltpu.VMEM((tiles, most - 1, rows, ch, cols), bf16),
            pltpu.VMEM((tiles, most - 1, rows, ch, cols), bf16),
            dma((tiles, most - 1, chunks)),
            dma((tiles, most - 1, chunks)),
            dma((tiles, most)),
            dma((tiles, most)),
            dma((tiles, most)),
            dma((tiles, most)),
            dma((2,)),
            dma((2,)),
            dma((rots - 1,)),
            dma((rots - 1,)),
            dma((tiles, most - 1, chunks)),
            dma((tiles, most - 1, chunks)),
        ],
        compiler_params=pltpu.CompilerParams(
            collective_id=0, has_side_effects=True, vmem_limit_bytes=48 * 2**20
        ),
        name="mixing_layers",
    )(coarse_in, taps, lift, lift_bias[:, None], filt, group_bias[:, None])
    return jnp.transpose(out, (2, 1, 0, 3))[None]


def solution(mesh):
    return jax.shard_map(
        functools.partial(shards, mesh.shape["rot"], mesh.shape["space"]),
        mesh=mesh,
        in_specs=(
            P(None, "space", None, None),
            P("rot", None, "space", None, None),
            P("rot", None, None, None),
            P(),
            P("rot", None, None, None),
            P(),
        ),
        out_specs=P("rot", None, "space", None, None),
        check_vma=False,
    )
```

time: 141 us -> 40.5 us (0.29)
  the two profiles are of different devices: /device:TPU:1 before, /device:TPU:0 now
where the time goes in v1:
time: 40.5 us; the launch traced here: 40.3 us
  Pallas kernels  33.5 us (83%)
  local copies, waits for them, and re-layouts  6.42 us (16%)
    pallas_call x1, Pallas kernels, shards(): pl.pallas_call(functools.partial(kernel, rots, spaces), out_shape=jax.Sha...  33.5 us
    unnamed x13, local copies, waits for them, and re-layouts  3.29 us
    broadcast_in_dim x1, local copies, waits for them, and re-layouts, shards(): return jnp.transpose(out, (2, 1, 0, 3))[None]  2.05 us

profile of v1, /device:TPU:0, one launch (start us, length us, event | category | flops | bytes accessed | tf_op | source)
XLA Modules:
  0.0 40.3 jit_solution(17337600949418248930)
XLA Ops:
  0.0 0.0 copy-start.3
  0.0 0.7 %copy-done.3 = bf16[1,9,64,4]{2,3,1,0:T(4,128)(2,1)S(1)} copy-done((bf16[1,9,64,4]{2,3,1,0:T(4,128)(2,1)S(1)}, bf16[1,9,64,4]{2,3,1,0:T(4,128)(2,1)}, u32[]{:S(2)}) %copy-start.3) | copy-done | bytes 4632
  0.7 0.0 copy-start.4
  0.7 0.0 copy-start.1
  0.7 0.1 copy.17.lift_ref
  0.8 0.5 %copy-done.4 = f32[64]{0:T(128)S(1)} copy-done((f32[64]{0:T(128)S(1)}, f32[64]{0:T(128)}, u32[]{:S(2)}) %copy-start.4) | copy-done | bytes 280
  1.4 0.0 copy-start.5
  1.4 0.1 copy.18.lift_bias_ref
  1.5 0.6 %copy-done.5 = f32[64]{0:T(128)S(1)} copy-done((f32[64]{0:T(128)S(1)}, f32[64]{0:T(128)}, u32[]{:S(2)}) %copy-start.5) | copy-done | bytes 280
  2.0 0.1 copy.19.group_bias_ref
  2.1 0.0 copy-done.1
  2.1 0.2 fusion
  2.3 0.3 maximum_bitcast_fusion
  2.7 0.0 copy-start
  2.7 0.1 reshape.12
  2.8 0.1 copy.15
  2.9 0.0 copy-start.2
  3.0 0.9 %copy-done.2 = bf16[1,9,64,64]{3,2,1,0:T(8,128)(2,1)S(1)} copy-done((bf16[1,9,64,64]{3,2,1,0:T(8,128)(2,1)S(1)}, bf16[1,9,64,64]{3,2,1,0:T(8,128)(2,1)}, u32[]{:S(2)}) %copy-start.2) | copy-done | bytes 73752
  3.9 0.1 copy.24
  4.0 0.2 reshape.15.filter_ref
  4.2 0.0 copy-done
  4.2 0.6 %copy.23 = bf16[1,64,16,2,256]{4,1,2,3,0:T(8,128)(2,1)S(1)} copy(bf16[1,64,16,2,256]{4,3,2,1,0:T(2,128)(2,1)S(1)} %copy-done) | data formatting | bytes 2097152 | tf_op args[1]
  4.8 33.5 %mixing_layers.1 = bf16[2,16,64,256]{3,2,1,0:T(8,128)(2,1)S(1)} custom-call(bf16[2,16,64,256]{3,2,1,0:T(8,128)(2,1)S(1)} %bitcast.30, bf16[16,16,512]{2,1,0:T(8,128)(2,1)S(1)} %pad.13.raster_ref, bf16[64,48]{1,0:T(8,128)(2,1)S(1)} %copy.17.lift_ref, f32[64,1]{1,0:T(8,128)S(1)} %copy.18.lift_bias_ref, bf16[192,192]{1,0:T(8,128)(2,1)S(1)} %reshape.15.filter_ref, ...), custom_call_target="tpu_custom_call" | custom-call | tf_op jit(solution)/shard_map/mixing_layers/pallas_call | solution.py:370
  38.2 2.1 %copy.20 = bf16[1,64,16,2,256]{4,3,2,1,0:T(2,128)(2,1)} copy(bf16[1,64,16,2,256]{4,1,2,3,0:T(8,128)(2,1)S(1)} %bitcast.29) | data formatting | bytes 2097152 | tf_op jit(solution)/shard_map/broadcast_in_dim | solution.py:401
  (3 shorter events, 0.1 us)
Async XLA Ops:
  0.0 0.7 %copy-start.3 = (bf16[1,9,64,4]{2,3,1,0:T(4,128)(2,1)S(1)}, bf16[1,9,64,4]{2,3,1,0:T(4,128)(2,1)}, u32[]{:S(2)}) copy-start(bf16[1,9,64,4]{2,3,1,0:T(4,128)(2,1)} %param.8) | copy-start | bytes 13828
  0.7 0.7 %copy-start.4 = (f32[64]{0:T(128)S(1)}, f32[64]{0:T(128)}, u32[]{:S(2)}) copy-start(f32[64]{0:T(128)} %param.9) | copy-start | bytes 772
  0.7 1.4 %copy-start.1 = (bf16[4,16,2,256]{3,2,1,0:T(2,128)(2,1)S(1)}, bf16[4,16,2,256]{3,2,1,0:T(2,128)(2,1)}, u32[]{:S(2)}) copy-start(bf16[4,16,2,256]{3,2,1,0:T(2,128)(2,1)} %param.6) | copy-start | bytes 196612
  1.4 0.7 %copy-start.5 = (f32[64]{0:T(128)S(1)}, f32[64]{0:T(128)}, u32[]{:S(2)}) copy-start(f32[64]{0:T(128)} %param.11) | copy-start | bytes 772
  2.7 1.5 %copy-start = (bf16[1,64,16,2,256]{4,3,2,1,0:T(2,128)(2,1)S(1)}, bf16[1,64,16,2,256]{4,3,2,1,0:T(2,128)(2,1)}, u32[]{:S(2)}) copy-start(bf16[1,64,16,2,256]{4,3,2,1,0:T(2,128)(2,1)} %param.7) | copy-start | bytes 3145732
  2.9 1.0 %copy-start.2 = (bf16[1,9,64,64]{3,2,1,0:T(8,128)(2,1)S(1)}, bf16[1,9,64,64]{3,2,1,0:T(8,128)(2,1)}, u32[]{:S(2)}) copy-start(bf16[1,9,64,64]{3,2,1,0:T(8,128)(2,1)} %param.10) | copy-start | bytes 221188
